TPU v7x, 256 devices: a whole 4x4x8 slice. The times are simulated.
256 devices in a mesh: img: 64 (over z, x, core), hid: 4 (over y).
Axes of the slice: x: 4, y: 4, z: 8, core: 2. Of those that a mesh axis runs over, the one named last changes fastest.
Arguments:
- patches: bfloat16 [32768, 6144], P('img'), may hold values from -6 to 6
- hidden_grads: bfloat16 [32768, 24576], P('img', 'hid'), may hold values from -0.5 to 0.5
- proj_in: bfloat16 [6144, 128], replicated, may hold values from -0.078125 to 0.078125
- proj_out: bfloat16 [24576, 128], P('hid'), may hold values from -0.0390625 to 0.0390625
- slot_image: int32 [128], P('img'), may hold values from 0 to 127, each once
- patch_counts: int32 [128], P('img'), may hold values from 128 to 256, as said below
Outputs:
- sketches: float32 [16384, 128], P(('img', 'hid'))
Inputs may be any that keep to these rules, and one draw needn't show every extreme that they name: `slot_image`: each value names one image's slot; every image has exactly one slot. `patch_counts`: the counts of one packing block sum to at most 512; some block is full.
All inputs are finite; a program needn't handle non-finite values.
Results may differ from a plain program's by a relative error of at most 0.0003.
Values sent between devices are 32-bit elements; how exact they have to be, the bound alone decides.
A program may use at most 128 MiB of HBM per device.

v0:
```python
import jax
import jax.numpy as jnp
from jax import lax
from jax.sharding import PartitionSpec as P


def body(patches, hidden_grads, proj_in, proj_out, slot_image, patch_counts):
    rows = patches.shape[0]
    slots = slot_image.shape[0]
    width = proj_in.shape[1]
    groups = lax.axis_size("img")
    total = slots * groups
    reduced = jnp.dot(patches, proj_in, preferred_element_type=jnp.float32)
    projected = jnp.dot(hidden_grads, proj_out, preferred_element_type=jnp.float32)
    starts = jnp.cumsum(patch_counts) - patch_counts
    position = jnp.arange(rows, dtype=jnp.int32)
    member = (
        (position[None, :] >= starts[:, None])
        & (position[None, :] < (starts + patch_counts)[:, None])
    ).astype(jnp.float32)
    masked = member[:, :, None] * reduced[None, :, :]
    local = jnp.einsum("srk,rl->skl", masked, projected, precision=lax.Precision.HIGHEST)
    placing = (jnp.arange(total, dtype=jnp.int32)[:, None] == slot_image[None, :]).astype(
        jnp.float32
    )
    whole = jnp.dot(
        placing, local.reshape(slots, width * width), precision=lax.Precision.HIGHEST
    ).reshape(total * width, width)
    return lax.psum_scatter(whole, ("img", "hid"), scatter_dimension=0, tiled=True)


def solution(mesh):
    in_specs = (P("img", None), P("img", "hid"), P(), P("hid", None), P("img"), P("img"))
    out_specs = P(("img", "hid"), None)
    return jax.shard_map(body, mesh=mesh, in_specs=in_specs, out_specs=out_specs, check_vma=False)
```

profile of v0, /device:TPU:1, one launch (start us, length us, event | category | flops | bytes accessed | tf_op | source)
XLA Modules:
  0.0 1314.6 jit_solution(10809156701595667765)
XLA Ops:
  6.5 0.0 copy-start
  6.5 0.0 copy-start.2
  6.5 0.0 reduce-scatter.2.cloned.1.call-start
  6.5 1.0 reduce-window.8
  7.5 0.0 slice-start
  7.5 0.8 bitcast_subtract_fusion
  8.3 0.1 and_convert_fusion
  8.4 0.0 copy-done
  8.4 0.0 slice-start.1
  8.4 5.3 fusion.7
  13.7 0.0 copy-done.2
  13.7 0.0 slice-done
  13.7 0.0 slice-done.1
  13.7 0.0 copy-start.1
  13.8 1.8 convolution_bitcast_fusion
  15.6 0.6 convolution_bitcast_fusion.1
  16.2 0.0 copy-done.1
  16.2 5.6 fusion.3
  21.8 9.2 reshape.78
  31.1 0.0 reduce-scatter.2.cloned.1.call-update
  31.1 1276.7 %reduce-scatter.2.cloned.1.call-done = f32[64,128]{1,0:T(8,128)} async-done(((f32[16384,128]{1,0:T(8,128)}), f32[64,128]{1,0:T(8,128)}) %reduce-scatter.2.cloned.1.call-update) | async-done | bytes 32784 | tf_op jit(solution)/shard_map/reduce_scatter | solution.py:29
  (1 shorter events, 0.0 us)
Async XLA Ops:
  6.5 1.9 copy-start
  6.5 7.2 copy-start.2
  6.5 1301.2 %reduce-scatter.2.cloned.1.call-start = ((), (), s32[]{:S(2)}) async-start(), calls=%async_computation.1 | async-start | bytes 8421376 | tf_op jit(solution)/shard_map/reduce_scatter | solution.py:29
  7.5 6.2 slice-start
  8.4 5.3 slice-start.1
  13.7 2.4 copy-start.1
Sparse Core Ops, SparseCore 0:
  31.2 1276.5 reduce-scatter.1
where the time goes:
time: 1320 us; the launch traced here: 1310 us
  waiting for transfers between devices  1280 us (97%)
  between operations  13.5 us (1%)
  matrix products  13.3 us (1%)
    reduce_scatter x1, waiting for transfers between devices, body(): lax.psum_scatter(whole, ('img', 'hid'), scatter_dimension=0, tiled=True)  1280 us
  transfers between devices with their start and end apart: 1, of which 1 were waited for; matrix products, arithmetic and copies ran while one was open for 0% of the time, Pallas kernels for 0%

commit v1 on v0

v1 whole, which is shorter than its diff:
```python
import functools

import jax
import jax.numpy as jnp
from jax import lax
from jax.experimental import pallas as pl
from jax.experimental.pallas import tpu as pltpu
from jax.sharding import PartitionSpec as P

MESH = pl.DeviceIdType.MESH
XC = 8
CHUNK = 128


def far_first(n):
    return sorted(range(1, n), key=lambda o: -min(o, n - o))


def split(v):
    hi = v.astype(jnp.bfloat16)
    lo = (v - hi.astype(jnp.float32)).astype(jnp.bfloat16)
    return hi, lo


def kernel(nz, ny, image_ref, count_ref, x_hbm, g_hbm, wi_hbm, wo_hbm, out_ref,
           xv, gv, wi, wo, red, prj, part, gath, ring, pick, idrow, idxc, idz, where_smem,
           x_sem, g_sem, w_sem, id_send, id_recv, idz_send, idz_recv,
           p1_send, p1_recv, ag_send, ag_recv, p3_send, p3_recv):
    b, y = lax.axis_index("img"), lax.axis_index("hid")
    z, xc = b // XC, b % XC
    rows, depth = xv.shape
    kw, lw = wi.shape[1], wo.shape[1]
    half_rows = rows // 2
    npiece = ny * XC
    t = kw // npiece
    chunks = rows // CHUNK
    f32 = jnp.float32

    def dev(zz, cc, yy):
        return (zz * XC + cc, yy)

    loads = []
    w_in = pltpu.make_async_copy(wi_hbm, wi, w_sem.at[0])
    w_out = pltpu.make_async_copy(wo_hbm, wo, w_sem.at[1])

    def x_copy(i):
        return pltpu.make_async_copy(x_hbm.at[pl.ds(i * CHUNK, CHUNK)], xv.at[pl.ds(i * CHUNK, CHUNK)], x_sem.at[i])

    def g_copy(i):
        return pltpu.make_async_copy(g_hbm.at[pl.ds(i * CHUNK, CHUNK)], gv.at[pl.ds(i * CHUNK, CHUNK)], g_sem.at[i])

    w_in.start()
    x_copy(0).start()
    w_out.start()
    g_copy(0).start()
    for i in range(1, chunks):
        x_copy(i).start()
        g_copy(i).start()

    group = [(oc, oy) for oy in [0] + far_first(ny) for oc in [0] + far_first(XC) if (oc, oy) != (0, 0)]
    group.sort(key=lambda o: -(min(o[0] // 2, XC // 2 - o[0] // 2) + min(o[1], ny - o[1])))
    barrier = pltpu.get_barrier_semaphore()
    for oc, oy in group:
        pl.semaphore_signal(barrier, inc=1, device_id=dev(z, (xc + oc) % XC, (y + oy) % ny), device_id_type=MESH)
    for oz in far_first(nz):
        pl.semaphore_signal(barrier, inc=1, device_id=dev((z + oz) % nz, xc, y), device_id_type=MESH)

    slots = 2 * nz * XC
    lane = lax.broadcasted_iota(jnp.int32, (8, 128), 1)
    first, second = image_ref[0], image_ref[1]
    idrow[...] = jnp.where(lane == b, first, jnp.where(lane == slots // 2 + b, second, 0))

    c0, c1 = count_ref[0], count_ref[1]

    def project(i):
        r = pl.ds(pl.multiple_of(i * CHUNK, CHUNK), CHUNK)
        x_copy(i).wait()
        red[r, :] = jnp.dot(xv[r, :], wi[...], preferred_element_type=f32)
        g_copy(i).wait()
        prj[r, :] = jnp.dot(gv[r, :], wo[...], preferred_element_type=f32)

    def members(h):
        pos = lax.broadcasted_iota(jnp.int32, (half_rows, lw), 0) + h * half_rows
        return pos < c0, (pos >= c0) & (pos < c0 + c1)

    def sketch(h, masks):
        r = pl.ds(h * half_rows, half_rows)
        a = jnp.concatenate(split(red[r, :].T), axis=0)
        hi, lo = split(prj[r, :])
        zero = jnp.zeros_like(hi)
        rhs = jnp.concatenate([jnp.where(m, v, zero) for m in masks for v in (hi, lo)], axis=1)
        full = jnp.dot(a, rhs, preferred_element_type=f32)
        return [
            full[:kw, 2 * lw * j : 2 * lw * j + lw]
            + (full[:kw, 2 * lw * j + lw : 2 * lw * (j + 1)] + full[kw:, 2 * lw * j : 2 * lw * j + lw])
            for j in range(len(masks))
        ]

    def put(s, value):
        for i in range(npiece):
            part[s, i] = value[i * t : (i + 1) * t]

    def scatter(s):
        pltpu.make_async_copy(part.at[s, y * XC + xc], gath.at[s, y, xc], p1_recv.at[s]).start()
        for oc, oy in group:
            cc, yy = (xc + oc) % XC, (y + oy) % ny
            pltpu.make_async_remote_copy(
                src_ref=part.at[s, yy * XC + cc], dst_ref=gath.at[s, y, xc],
                send_sem=p1_send.at[s], recv_sem=p1_recv.at[s],
                device_id=dev(z, cc, yy), device_id_type=MESH).start()

    def spread(s):
        pltpu.make_async_copy(gath.at[s], gath.at[s], p1_recv.at[s]).wait()
        total = gath[s, 0]
        for j in range(1, ny):
            total = total + gath[s, j]
        ring[s, z] = total
        for oz in far_first(nz):
            pltpu.make_async_remote_copy(
                src_ref=ring.at[s, z], dst_ref=ring.at[s, z],
                send_sem=ag_send.at[s], recv_sem=ag_recv.at[s],
                device_id=dev((z + oz) % nz, xc, y), device_id_type=MESH).start()

    w_in.wait()
    x_copy(0).wait()
    red[pl.ds(0, CHUNK), :] = jnp.dot(xv[pl.ds(0, CHUNK), :], wi[...], preferred_element_type=f32)

    pl.semaphore_wait(barrier, len(group) + nz - 1)
    idxc[xc] = idrow[...]
    for oc in far_first(XC):
        pltpu.make_async_remote_copy(
            src_ref=idrow, dst_ref=idxc.at[xc], send_sem=id_send, recv_sem=id_recv,
            device_id=dev(z, (xc + oc) % XC, y), device_id_type=MESH).start()

    w_out.wait()
    g_copy(0).wait()
    prj[pl.ds(0, CHUNK), :] = jnp.dot(gv[pl.ds(0, CHUNK), :], wo[...], preferred_element_type=f32)

    def step(i, _):
        project(i)
        return 0

    lax.fori_loop(1, chunks // 2, step, 0)
    s0, s1 = sketch(0, members(0))
    put(0, s0)
    scatter(0)

    pltpu.make_async_copy(idxc.at[pl.ds(0, XC - 1)], idxc.at[pl.ds(0, XC - 1)], id_recv).wait()
    ids = idxc[0]
    for j in range(1, XC):
        ids = ids + idxc[j]
    idz[z] = ids
    for oz in far_first(nz):
        pltpu.make_async_remote_copy(
            src_ref=idz.at[z], dst_ref=idz.at[z], send_sem=idz_send, recv_sem=idz_recv,
            device_id=dev((z + oz) % nz, xc, y), device_id_type=MESH).start()

    lax.fori_loop(chunks // 2, chunks, step, 0)
    put(1, s1 + sketch(1, members(1)[1:])[0])
    scatter(1)

    spread(0)
    pltpu.make_async_copy(idz.at[pl.ds(0, nz - 1)], idz.at[pl.ds(0, nz - 1)], idz_recv).wait()
    ids = idz[0]
    for j in range(1, nz):
        ids = ids + idz[j]
    for i in range(2 * XC):
        hit = jnp.where((ids == 2 * XC * z + i) & (lane < slots), lane, 0)
        where_smem[i] = jnp.max(hit)
    spread(1)

    for s in range(2):
        pltpu.make_async_copy(ring.at[s, pl.ds(0, nz - 1)], ring.at[s, pl.ds(0, nz - 1)], ag_recv.at[s]).wait()

    side, place = y // 2, (y % 2) * XC + xc
    for oc in far_first(XC) + [0]:
        cc = (xc + oc) % XC
        for p in range(2):
            yy = 2 * p + side
            src = where_smem[2 * cc + p]
            s, rest = src // (slots // 2), src % (slots // 2)
            pick[2 * cc + p] = ring[s, rest // XC, rest % XC]
            if oc == 0:
                @pl.when(yy == y)
                def _():
                    pltpu.make_async_copy(pick.at[2 * cc + p], out_ref.at[place], p3_recv).start()

                @pl.when(yy != y)
                def _():
                    pltpu.make_async_remote_copy(
                        src_ref=pick.at[2 * cc + p], dst_ref=out_ref.at[place],
                        send_sem=p3_send, recv_sem=p3_recv,
                        device_id=dev(z, cc, yy), device_id_type=MESH).start()
            else:
                pltpu.make_async_remote_copy(
                    src_ref=pick.at[2 * cc + p], dst_ref=out_ref.at[place],
                    send_sem=p3_send, recv_sem=p3_recv,
                    device_id=dev(z, cc, yy), device_id_type=MESH).start()

    def sent(ref, sem):
        pltpu.make_async_copy(ref, ref, sem).wait()

    sent(idxc.at[pl.ds(0, XC - 1)], id_send)
    sent(idz.at[pl.ds(0, nz - 1)], idz_send)
    for s in range(2):
        sent(part.at[s, pl.ds(0, npiece - 1)], p1_send.at[s])
        sent(ring.at[s, pl.ds(0, nz - 1)], ag_send.at[s])
    own = (y == side) | (y == 2 + side)

    @pl.when(own)
    def _():
        sent(pick.at[pl.ds(0, 2 * XC - 1)], p3_send)

    @pl.when(jnp.logical_not(own))
    def _():
        sent(pick, p3_send)

    pltpu.make_async_copy(out_ref, out_ref, p3_recv).wait()


def body(nz, ny, patches, hidden_grads, proj_in, proj_out, slot_image, patch_counts):
    rows, depth = patches.shape
    hidden = hidden_grads.shape[1]
    kw, lw = proj_in.shape[1], proj_out.shape[1]
    t = kw // (ny * XC)
    chunks = rows // CHUNK
    f32, i32, bf16 = jnp.float32, jnp.int32, jnp.bfloat16
    dma = pltpu.SemaphoreType.DMA
    out = pl.pallas_call(
        functools.partial(kernel, nz, ny),
        out_shape=jax.ShapeDtypeStruct((2 * XC, t, lw), f32),
        in_specs=[pl.BlockSpec(memory_space=pltpu.SMEM)] * 2 + [pl.BlockSpec(memory_space=pltpu.HBM)] * 4,
        out_specs=pl.BlockSpec(memory_space=pltpu.VMEM),
        scratch_shapes=[
            pltpu.VMEM((rows, depth), bf16), pltpu.VMEM((rows, hidden), bf16),
            pltpu.VMEM((depth, kw), bf16), pltpu.VMEM((hidden, lw), bf16),
            pltpu.VMEM((rows, kw), f32), pltpu.VMEM((rows, lw), f32),
            pltpu.VMEM((2, ny * XC, t, lw), f32),
            pltpu.VMEM((2, ny, XC, t, lw), f32),
            pltpu.VMEM((2, nz, XC, t, lw), f32),
            pltpu.VMEM((2 * XC, t, lw), f32),
            pltpu.VMEM((8, 128), i32), pltpu.VMEM((XC, 8, 128), i32), pltpu.VMEM((nz, 8, 128), i32),
            pltpu.SMEM((2 * XC,), i32),
            dma((chunks,)), dma((chunks,)), dma((2,)), dma, dma, dma, dma,
            dma((2,)), dma((2,)), dma((2,)), dma((2,)), dma, dma,
        ],
        name="sketch",
        compiler_params=pltpu.CompilerParams(collective_id=0, has_side_effects=True, vmem_limit_bytes=56 << 20),
    )(slot_image, patch_counts, patches, hidden_grads, proj_in, proj_out)
    return out.reshape(2 * XC * t, lw)


def solution(mesh):
    ny = mesh.shape["hid"]
    nz = mesh.shape["img"] // XC
    in_specs = (P("img", None), P("img", "hid"), P(), P("hid", None), P("img"), P("img"))
    return jax.shard_map(
        functools.partial(body, nz, ny), mesh=mesh, in_specs=in_specs,
        out_specs=P(("img", "hid"), None), check_vma=False)
```

time: 1320 us -> 34.2 us (0.03)
  waiting for transfers between devices: 1280 us -> 0 us
  Pallas kernels: 0 us -> 32.7 us
  between operations: 13.5 us -> 0.01 us
  matrix products: 13.3 us -> 0 us
    reduce_scatter x1 -> x0, waiting for transfers between devices: 1280 us -> none  [body(): lax.psum_scatter(whole, ('img', 'hid'), scatter_dimension=0, tiled=True)]
    pallas_call x0 -> x1, Pallas kernels: none -> 32.7 us  [body(): pl.pallas_call(functools.partial(kernel, nz, ny), out_shape=jax.ShapeDtyp...]
    dot_general x4 -> x0, matrix products: 13.3 us -> none  [the longest x1 5.65 us: body(): jnp.dot(placing, local.reshape(slots, width * width), precision=lax.Preci...]
  transfers between devices with their start and end apart: 1 -> 0, of which waited for: 1 -> 0; matrix products, arithmetic and copies ran while one was open for 0% -> 0% of each run, Pallas kernels for 0% -> 0%
where the time goes in v1:
time: 34.2 us; the launch traced here: 34.1 us
  Pallas kernels  32.7 us (96%)
  local copies, waits for them, and re-layouts  1.38 us (4%)
    pallas_call x1, Pallas kernels, body(): pl.pallas_call(functools.partial(kernel, nz, ny), out_shape=jax.ShapeDtyp...  32.7 us
    unnamed x1, local copies, waits for them, and re-layouts  1.38 us

profile of v1, /device:TPU:1, one launch (start us, length us, event | category | flops | bytes accessed | tf_op | source)
XLA Modules:
  0.0 34.1 jit_solution(1002803244214657847)
XLA Ops:
  0.0 32.7 %sketch.1 = f32[16,4,128]{2,1,0:T(4,128)} custom-call(s32[2]{0:T(128)} %image_ref.1, s32[2]{0:T(128)} %count_ref.1, bf16[512,6144]{1,0:T(8,128)(2,1)} %x_hbm.1, bf16[512,6144]{1,0:T(8,128)(2,1)} %g_hbm.1, bf16[6144,128]{1,0:T(8,128)(2,1)} %wi_hbm.1, bf16[6144,128]{1,0:T(8,128)(2,1)} %wo_hbm.1), custom_call_target="tpu_custom_call" | custom-call | tf_op jit(solution)/shard_map/sketch/pallas_call | solution.py:229
  32.7 1.4 %copy.8 = f32[64,128]{1,0:T(8,128)} copy(f32[64,128]{1,0:T(8,128)} %bitcast.1) | data formatting | bytes 65536

commit v2 on v0

v2 whole, which is shorter than its diff:
```python
import functools

import jax
import jax.numpy as jnp
from jax import lax
from jax.experimental import pallas as pl
from jax.experimental.pallas import tpu as pltpu
from jax.sharding import PartitionSpec as P

MESH = pl.DeviceIdType.MESH
XC = 8
CUTS = 4
AHEAD = 3


def far_first(n):
    return sorted(range(1, n), key=lambda o: -min(o, n - o))


def middle_out(j, n):
    return n // 2 + lax.div(j + 1, 2) * (1 - 2 * lax.rem(j, 2))


def split(v):
    hi = v.astype(jnp.bfloat16)
    lo = (v - hi.astype(jnp.float32)).astype(jnp.bfloat16)
    return hi, lo


def kernel(nz, ny, image_ref, count_ref, x_hbm, g_hbm, wi_hbm, wo_hbm, out_ref,
           xv, gv, wi, wo, red, prj, later, part, gath, ring, pick, idrow, idxc, idz, where_smem,
           x_sem, g_sem, wi_sem, wo_sem, id_send, id_recv, idz_send, idz_recv,
           p1_send, p1_recv, ag_send, ag_recv, p3_send, p3_recv):
    b, y = lax.axis_index("img"), lax.axis_index("hid")
    z, xc = lax.div(b, XC), lax.rem(b, XC)
    rows, depth = xv.shape
    kw, lw = wi.shape[1], wo.shape[1]
    half_rows, cols = rows // 2, depth // CUTS
    npiece = ny * XC
    t = kw // npiece
    slots = 2 * nz * XC
    f32 = jnp.float32

    def at_z(o):
        return (lax.rem(z + o, nz) * XC + xc, y)

    def at_xc(o):
        return lax.rem(xc + o, XC)

    def row_part(h):
        return pl.ds(pl.multiple_of(h * half_rows, half_rows), half_rows)

    def col_part(q):
        return pl.ds(pl.multiple_of(q * cols, cols), cols)

    def rows_in(h, q):
        r, c = row_part(h), col_part(q)
        return (
            pltpu.make_async_copy(x_hbm.at[r, c], xv.at[r, c], x_sem.at[h, q]),
            pltpu.make_async_copy(g_hbm.at[r, c], gv.at[r, c], g_sem.at[h, q]),
        )

    def weights_in(q):
        c = col_part(q)
        return (
            pltpu.make_async_copy(wi_hbm.at[c], wi.at[c], wi_sem.at[q]),
            pltpu.make_async_copy(wo_hbm.at[c], wo.at[c], wo_sem.at[q]),
        )

    for q in range(AHEAD):
        (x_in, g_in), (a_in, o_in) = rows_in(0, q), weights_in(q)
        a_in.start()
        x_in.start()
        o_in.start()
        g_in.start()

    barrier = pltpu.get_barrier_semaphore()

    def greet(i, _):
        o = i + 1
        to = (z * XC + lax.rem(xc + lax.rem(o, XC), XC), lax.rem(y + lax.div(o, XC), ny))
        pl.semaphore_signal(barrier, inc=1, device_id=to, device_id_type=MESH)
        return 0

    lax.fori_loop(0, npiece - 1, greet, 0)
    for o in range(1, nz):
        pl.semaphore_signal(barrier, inc=1, device_id=at_z(o), device_id_type=MESH)

    lane = lax.broadcasted_iota(jnp.int32, (8, 128), 1)
    first, second = image_ref[0], image_ref[1]
    idrow[...] = jnp.where(lane == b, first, jnp.where(lane == slots // 2 + b, second, 0))
    c0, c1 = count_ref[0], count_ref[1]

    def sketch(a, h, start, count):
        pos = lax.broadcasted_iota(jnp.int32, (half_rows, lw), 0) + h * half_rows
        hi, lo = split(jnp.where((pos >= start) & (pos < start + count), prj[...], 0.0))
        full = jnp.dot(a, jnp.concatenate([hi, lo], axis=1), preferred_element_type=f32)
        return full[:kw, :lw] + (full[:kw, lw:] + full[kw:, :lw])

    def send_piece(s, cc, yy):
        pltpu.make_async_remote_copy(
            src_ref=part.at[s, yy * XC + cc], dst_ref=gath.at[s, y, xc],
            send_sem=p1_send.at[s], recv_sem=p1_recv.at[s, xc],
            device_id=(z * XC + cc, yy), device_id_type=MESH).start()

    later[...] = jnp.zeros_like(later)

    def half(h, _):
        def step(q, _):
            for c in rows_in(h, q):
                c.wait()

            @pl.when(h == 0)
            def _():
                for c in weights_in(q):
                    c.wait()

            n = h * CUTS + q + AHEAD

            @pl.when(n < 2 * CUTS)
            def _():
                hh, qq = lax.div(n, CUTS), lax.rem(n, CUTS)

                @pl.when(hh == 0)
                def _():
                    for c in weights_in(qq):
                        c.start()

                for c in rows_in(hh, qq):
                    c.start()

            @pl.when(q == 0)
            def _():
                red[...] = jnp.zeros_like(red)
                prj[...] = jnp.zeros_like(prj)

            r, c = row_part(h), col_part(q)
            red[...] += jnp.dot(xv[r, c], wi[c, :], preferred_element_type=f32)
            prj[...] += jnp.dot(gv[r, c], wo[c, :], preferred_element_type=f32)
            return 0

        lax.fori_loop(0, CUTS, step, 0)
        a = jnp.concatenate(split(red[...].T), axis=0)
        value = later[...] + sketch(a, h, jnp.where(h == 0, 0, c0), jnp.where(h == 0, c0, c1))
        for i in range(npiece):
            part[h, i] = value[i * t : (i + 1) * t]

        @pl.when(h == 0)
        def _():
            pl.semaphore_wait(barrier, npiece + nz - 2)

        def to_row(j, _):
            yy = lax.rem(y + middle_out(j, ny), ny)
            for o in far_first(XC):
                send_piece(h, at_xc(o), yy)

            @pl.when(yy != y)
            def _():
                send_piece(h, xc, yy)

            return 0

        lax.fori_loop(0, ny, to_row, 0)
        pltpu.make_async_copy(part.at[h, y * XC + xc], gath.at[h, y, xc], p1_recv.at[h, xc]).start()

        @pl.when(h == 0)
        def _():
            for o in far_first(XC):
                pltpu.make_async_remote_copy(
                    src_ref=idrow, dst_ref=idxc.at[xc], send_sem=id_send, recv_sem=id_recv,
                    device_id=(z * XC + at_xc(o), y), device_id_type=MESH).start()
            idxc[xc] = idrow[...]
            later[...] = sketch(a, 0, c0, c1)

        return 0

    lax.fori_loop(0, 2, half, 0)

    def spread(s):
        def one(j, _):
            src = at_xc(XC - middle_out(XC - 1 - j, XC))
            pltpu.make_async_copy(gath.at[s, :, 0], gath.at[s, :, 0], p1_recv.at[s, src]).wait()
            total = gath[s, 0, src]
            for i in range(1, ny):
                total = total + gath[s, i, src]
            ring[s, z, src] = total
            for o in far_first(nz):
                pltpu.make_async_remote_copy(
                    src_ref=ring.at[s, z, src], dst_ref=ring.at[s, z, src],
                    send_sem=ag_send.at[s], recv_sem=ag_recv.at[s],
                    device_id=at_z(o), device_id_type=MESH).start()
            return 0

        lax.fori_loop(0, XC, one, 0)

    def add_ids(s, _):
        @pl.when(s == 1)
        def _():
            pltpu.make_async_copy(idxc.at[pl.ds(0, XC - 1)], idxc.at[pl.ds(0, XC - 1)], id_recv).wait()
            ids = idxc[0]
            for j in range(1, XC):
                ids = ids + idxc[j]
            idz[z] = ids
            for o in far_first(nz):
                pltpu.make_async_remote_copy(
                    src_ref=idz.at[z], dst_ref=idz.at[z], send_sem=idz_send, recv_sem=idz_recv,
                    device_id=at_z(o), device_id_type=MESH).start()

        spread(s)
        return 0

    lax.fori_loop(0, 2, add_ids, 0)

    pltpu.make_async_copy(idz.at[pl.ds(0, nz - 1)], idz.at[pl.ds(0, nz - 1)], idz_recv).wait()
    ids = idz[0]
    for j in range(1, nz):
        ids = ids + idz[j]
    for i in range(2 * XC):
        where_smem[i] = jnp.max(jnp.where((ids == 2 * XC * z + i) & (lane < slots), lane, 0))

    def sent(ref, sem):
        pltpu.make_async_copy(ref, ref, sem).wait()

    sent(idxc.at[pl.ds(0, XC - 1)], id_send)
    sent(idz.at[pl.ds(0, nz - 1)], idz_send)
    for s in range(2):
        sent(part.at[s, pl.ds(0, npiece - 1)], p1_send.at[s])
    for s in range(2):
        pltpu.make_async_copy(ring.at[s, pl.ds(0, nz - 1)], ring.at[s, pl.ds(0, nz - 1)], ag_recv.at[s]).wait()

    side = lax.div(y, 2)
    place = lax.rem(y, 2) * XC + xc

    def take(i):
        src = where_smem[i]
        pick[i] = ring[lax.div(src, slots // 2), lax.rem(lax.div(src, XC), nz), lax.rem(src, XC)]

    def deliver(i, cc, yy):
        pltpu.make_async_remote_copy(
            src_ref=pick.at[i], dst_ref=out_ref.at[place], send_sem=p3_send, recv_sem=p3_recv,
            device_id=(z * XC + cc, yy), device_id_type=MESH).start()

    def to_owner(j, _):
        cc = at_xc(middle_out(j, XC))
        for p in range(2):
            take(2 * cc + p)
            deliver(2 * cc + p, cc, 2 * p + side)
        return 0

    lax.fori_loop(0, XC - 1, to_owner, 0)
    for p in range(2):
        yy = 2 * p + side
        take(2 * xc + p)

        @pl.when(yy == y)
        def _():
            pltpu.make_async_copy(pick.at[2 * xc + p], out_ref.at[place], p3_recv).start()

        @pl.when(yy != y)
        def _():
            deliver(2 * xc + p, xc, yy)

    for s in range(2):
        sent(ring.at[s, pl.ds(0, nz - 1)], ag_send.at[s])
    own = (y == side) | (y == 2 + side)

    @pl.when(own)
    def _():
        sent(pick.at[pl.ds(0, 2 * XC - 1)], p3_send)

    @pl.when(jnp.logical_not(own))
    def _():
        sent(pick, p3_send)

    pltpu.make_async_copy(out_ref, out_ref, p3_recv).wait()


def body(nz, ny, patches, hidden_grads, proj_in, proj_out, slot_image, patch_counts):
    rows, depth = patches.shape
    hidden = hidden_grads.shape[1]
    kw, lw = proj_in.shape[1], proj_out.shape[1]
    t = kw // (ny * XC)
    f32, i32, bf16 = jnp.float32, jnp.int32, jnp.bfloat16
    dma = pltpu.SemaphoreType.DMA
    out = pl.pallas_call(
        functools.partial(kernel, nz, ny),
        out_shape=jax.ShapeDtypeStruct((2 * XC, t, lw), f32),
        in_specs=[pl.BlockSpec(memory_space=pltpu.SMEM)] * 2 + [pl.BlockSpec(memory_space=pltpu.HBM)] * 4,
        out_specs=pl.BlockSpec(memory_space=pltpu.HBM),
        scratch_shapes=[
            pltpu.VMEM((rows, depth), bf16), pltpu.VMEM((rows, hidden), bf16),
            pltpu.VMEM((depth, kw), bf16), pltpu.VMEM((hidden, lw), bf16),
            pltpu.VMEM((rows // 2, kw), f32), pltpu.VMEM((rows // 2, lw), f32), pltpu.VMEM((kw, lw), f32),
            pltpu.VMEM((2, ny * XC, t, lw), f32),
            pltpu.VMEM((2, ny, XC, t, lw), f32),
            pltpu.VMEM((2, nz, XC, t, lw), f32),
            pltpu.VMEM((2 * XC, t, lw), f32),
            pltpu.VMEM((8, 128), i32), pltpu.VMEM((XC, 8, 128), i32), pltpu.VMEM((nz, 8, 128), i32),
            pltpu.SMEM((2 * XC,), i32),
            dma((2, CUTS)), dma((2, CUTS)), dma((CUTS,)), dma((CUTS,)), dma, dma, dma, dma,
            dma((2,)), dma((2, XC)), dma((2,)), dma((2,)), dma, dma,
        ],
        name="sketch",
        compiler_params=pltpu.CompilerParams(collective_id=0, has_side_effects=True, vmem_limit_bytes=56 << 20),
    )(slot_image, patch_counts, patches, hidden_grads, proj_in, proj_out)
    return out.reshape(2 * XC * t, lw)


def solution(mesh):
    ny = mesh.shape["hid"]
    nz = mesh.shape["img"] // XC
    in_specs = (P("img", None), P("img", "hid"), P(), P("hid", None), P("img"), P("img"))
    return jax.shard_map(
        functools.partial(body, nz, ny), mesh=mesh, in_specs=in_specs,
        out_specs=P(("img", "hid"), None), check_vma=False)
```

time: 1320 us -> 32.8 us (0.02)
  waiting for transfers between devices: 1280 us -> 0 us
  Pallas kernels: 0 us -> 31.3 us
  between operations: 13.5 us -> 0.01 us
  matrix products: 13.3 us -> 0 us
    reduce_scatter x1 -> x0, waiting for transfers between devices: 1280 us -> none  [body(): lax.psum_scatter(whole, ('img', 'hid'), scatter_dimension=0, tiled=True)]
    pallas_call x0 -> x1, Pallas kernels: none -> 31.3 us  [body(): pl.pallas_call(functools.partial(kernel, nz, ny), out_shape=jax.ShapeDtyp...]
    dot_general x4 -> x0, matrix products: 13.3 us -> none  [the longest x1 5.65 us: body(): jnp.dot(placing, local.reshape(slots, width * width), precision=lax.Preci...]
  transfers between devices with their start and end apart: 1 -> 0, of which waited for: 1 -> 0; matrix products, arithmetic and copies ran while one was open for 0% -> 0% of each run, Pallas kernels for 0% -> 0%
where the time goes in v2:
time: 32.8 us; the launch traced here: 32.6 us
  Pallas kernels  31.3 us (95%)
  local copies, waits for them, and re-layouts  1.38 us (4%)
    pallas_call x1, Pallas kernels, body(): pl.pallas_call(functools.partial(kernel, nz, ny), out_shape=jax.ShapeDtyp...  31.3 us
    unnamed x1, local copies, waits for them, and re-layouts  1.38 us

profile of v2, /device:TPU:1, one launch (start us, length us, event | category | flops | bytes accessed | tf_op | source)
XLA Modules:
  0.0 32.6 jit_solution(8854266289801135451)
XLA Ops:
  0.0 31.3 %sketch.1 = f32[16,4,128]{2,1,0:T(4,128)} custom-call(s32[2]{0:T(128)} %image_ref.1, s32[2]{0:T(128)} %count_ref.1, bf16[512,6144]{1,0:T(8,128)(2,1)} %x_hbm.1, bf16[512,6144]{1,0:T(8,128)(2,1)} %g_hbm.1, bf16[6144,128]{1,0:T(8,128)(2,1)} %wi_hbm.1, bf16[6144,128]{1,0:T(8,128)(2,1)} %wo_hbm.1), custom_call_target="tpu_custom_call" | custom-call | tf_op jit(solution)/shard_map/sketch/pallas_call | solution.py:285
  31.3 1.4 %copy.8 = f32[64,128]{1,0:T(8,128)} copy(f32[64,128]{1,0:T(8,128)} %bitcast.1) | data formatting | bytes 65536

commit v3 on v2

--- a/solution.py
+++ b/solution.py
@@ -9,6 +9,7 @@
 
 MESH = pl.DeviceIdType.MESH
 XC = 8
+NEAR = 2
 CUTS = 4
 AHEAD = 3
 
@@ -36,7 +37,8 @@
     rows, depth = xv.shape
     kw, lw = wi.shape[1], wo.shape[1]
     half_rows, cols = rows // 2, depth // CUTS
-    npiece = ny * XC
+    npiece = ny * NEAR
+    block, here = lax.div(xc, NEAR), lax.rem(xc, NEAR)
     t = kw // npiece
     slots = 2 * nz * XC
     f32 = jnp.float32
@@ -46,6 +48,12 @@
 
     def at_xc(o):
         return lax.rem(xc + o, XC)
+
+    def near(o):
+        return lax.rem(here + o, NEAR)
+
+    def to_near(k):
+        return z * XC + block * NEAR + k
 
     def row_part(h):
         return pl.ds(pl.multiple_of(h * half_rows, half_rows), half_rows)
@@ -82,13 +90,13 @@
         pl.semaphore_signal(barrier, inc=1, device_id=to, device_id_type=MESH)
         return 0
 
-    lax.fori_loop(0, npiece - 1, greet, 0)
+    lax.fori_loop(0, ny * XC - 1, greet, 0)
     for o in range(1, nz):
         pl.semaphore_signal(barrier, inc=1, device_id=at_z(o), device_id_type=MESH)
 
     lane = lax.broadcasted_iota(jnp.int32, (8, 128), 1)
     first, second = image_ref[0], image_ref[1]
-    idrow[...] = jnp.where(lane == b, first, jnp.where(lane == slots // 2 + b, second, 0))
+    idrow[...] = jnp.where(lane == b, first + 1, jnp.where(lane == slots // 2 + b, second + 1, 0))
     c0, c1 = count_ref[0], count_ref[1]
 
     def sketch(a, h, start, count):
@@ -97,11 +105,11 @@
         full = jnp.dot(a, jnp.concatenate([hi, lo], axis=1), preferred_element_type=f32)
         return full[:kw, :lw] + (full[:kw, lw:] + full[kw:, :lw])
 
-    def send_piece(s, cc, yy):
+    def send_piece(s, k, yy):
         pltpu.make_async_remote_copy(
-            src_ref=part.at[s, yy * XC + cc], dst_ref=gath.at[s, y, xc],
-            send_sem=p1_send.at[s], recv_sem=p1_recv.at[s, xc],
-            device_id=(z * XC + cc, yy), device_id_type=MESH).start()
+            src_ref=part.at[s, yy * NEAR + k], dst_ref=gath.at[s, y, here],
+            send_sem=p1_send.at[s], recv_sem=p1_recv.at[s, here],
+            device_id=(to_near(k), yy), device_id_type=MESH).start()
 
     later[...] = jnp.zeros_like(later)
 
@@ -147,29 +155,29 @@
 
         @pl.when(h == 0)
         def _():
-            pl.semaphore_wait(barrier, npiece + nz - 2)
+            pl.semaphore_wait(barrier, ny * XC + nz - 2)
 
         def to_row(j, _):
             yy = lax.rem(y + middle_out(j, ny), ny)
-            for o in far_first(XC):
-                send_piece(h, at_xc(o), yy)
+            for o in far_first(NEAR):
+                send_piece(h, near(o), yy)
 
             @pl.when(yy != y)
             def _():
-                send_piece(h, xc, yy)
+                send_piece(h, here, yy)
 
             return 0
 
         lax.fori_loop(0, ny, to_row, 0)
-        pltpu.make_async_copy(part.at[h, y * XC + xc], gath.at[h, y, xc], p1_recv.at[h, xc]).start()
+        pltpu.make_async_copy(part.at[h, y * NEAR + here], gath.at[h, y, here], p1_recv.at[h, here]).start()
 
         @pl.when(h == 0)
         def _():
-            for o in far_first(XC):
+            for o in far_first(NEAR):
                 pltpu.make_async_remote_copy(
-                    src_ref=idrow, dst_ref=idxc.at[xc], send_sem=id_send, recv_sem=id_recv,
-                    device_id=(z * XC + at_xc(o), y), device_id_type=MESH).start()
-            idxc[xc] = idrow[...]
+                    src_ref=idrow, dst_ref=idxc.at[here], send_sem=id_send, recv_sem=id_recv,
+                    device_id=(to_near(near(o)), y), device_id_type=MESH).start()
+            idxc[here] = idrow[...]
             later[...] = sketch(a, 0, c0, c1)
 
         return 0
@@ -178,7 +186,7 @@
 
     def spread(s):
         def one(j, _):
-            src = at_xc(XC - middle_out(XC - 1 - j, XC))
+            src = near(NEAR - middle_out(NEAR - 1 - j, NEAR))
             pltpu.make_async_copy(gath.at[s, :, 0], gath.at[s, :, 0], p1_recv.at[s, src]).wait()
             total = gath[s, 0, src]
             for i in range(1, ny):
@@ -191,14 +199,14 @@
                     device_id=at_z(o), device_id_type=MESH).start()
             return 0
 
-        lax.fori_loop(0, XC, one, 0)
+        lax.fori_loop(0, NEAR, one, 0)
 
     def add_ids(s, _):
         @pl.when(s == 1)
         def _():
-            pltpu.make_async_copy(idxc.at[pl.ds(0, XC - 1)], idxc.at[pl.ds(0, XC - 1)], id_recv).wait()
+            pltpu.make_async_copy(idxc.at[pl.ds(0, NEAR - 1)], idxc.at[pl.ds(0, NEAR - 1)], id_recv).wait()
             ids = idxc[0]
-            for j in range(1, XC):
+            for j in range(1, NEAR):
                 ids = ids + idxc[j]
             idz[z] = ids
             for o in far_first(nz):
@@ -216,12 +224,12 @@
     for j in range(1, nz):
         ids = ids + idz[j]
     for i in range(2 * XC):
-        where_smem[i] = jnp.max(jnp.where((ids == 2 * XC * z + i) & (lane < slots), lane, 0))
+        where_smem[i] = jnp.max(jnp.where(ids == 2 * XC * z + i + 1, lane, -1))
 
     def sent(ref, sem):
         pltpu.make_async_copy(ref, ref, sem).wait()
 
-    sent(idxc.at[pl.ds(0, XC - 1)], id_send)
+    sent(idxc.at[pl.ds(0, NEAR - 1)], id_send)
     sent(idz.at[pl.ds(0, nz - 1)], idz_send)
     for s in range(2):
         sent(part.at[s, pl.ds(0, npiece - 1)], p1_send.at[s])
@@ -229,15 +237,17 @@
         pltpu.make_async_copy(ring.at[s, pl.ds(0, nz - 1)], ring.at[s, pl.ds(0, nz - 1)], ag_recv.at[s]).wait()
 
     side = lax.div(y, 2)
-    place = lax.rem(y, 2) * XC + xc
+    place = lax.rem(y, 2) * NEAR + here
 
     def take(i):
-        src = where_smem[i]
-        pick[i] = ring[lax.div(src, slots // 2), lax.rem(lax.div(src, XC), nz), lax.rem(src, XC)]
+        found = where_smem[i]
+        src = jnp.maximum(found, 0)
+        piece = ring[lax.div(src, slots // 2), lax.rem(lax.div(src, XC), nz), lax.rem(src, NEAR)]
+        pick[i] = jnp.where(found >= 0, piece, 0.0)
 
     def deliver(i, cc, yy):
         pltpu.make_async_remote_copy(
-            src_ref=pick.at[i], dst_ref=out_ref.at[place], send_sem=p3_send, recv_sem=p3_recv,
+            src_ref=pick.at[i], dst_ref=out_ref.at[block, place], send_sem=p3_send, recv_sem=p3_recv,
             device_id=(z * XC + cc, yy), device_id_type=MESH).start()
 
     def to_owner(j, _):
@@ -254,7 +264,7 @@
 
         @pl.when(yy == y)
         def _():
-            pltpu.make_async_copy(pick.at[2 * xc + p], out_ref.at[place], p3_recv).start()
+            pltpu.make_async_copy(pick.at[2 * xc + p], out_ref.at[block, place], p3_recv).start()
 
         @pl.when(yy != y)
         def _():
@@ -279,31 +289,31 @@
     rows, depth = patches.shape
     hidden = hidden_grads.shape[1]
     kw, lw = proj_in.shape[1], proj_out.shape[1]
-    t = kw // (ny * XC)
+    t = kw // (ny * NEAR)
     f32, i32, bf16 = jnp.float32, jnp.int32, jnp.bfloat16
     dma = pltpu.SemaphoreType.DMA
     out = pl.pallas_call(
         functools.partial(kernel, nz, ny),
-        out_shape=jax.ShapeDtypeStruct((2 * XC, t, lw), f32),
+        out_shape=pltpu.VMEM((XC // NEAR, 2 * NEAR, t, lw), f32),
         in_specs=[pl.BlockSpec(memory_space=pltpu.SMEM)] * 2 + [pl.BlockSpec(memory_space=pltpu.HBM)] * 4,
-        out_specs=pl.BlockSpec(memory_space=pltpu.HBM),
+        out_specs=pl.BlockSpec(memory_space=pltpu.VMEM),
         scratch_shapes=[
             pltpu.VMEM((rows, depth), bf16), pltpu.VMEM((rows, hidden), bf16),
             pltpu.VMEM((depth, kw), bf16), pltpu.VMEM((hidden, lw), bf16),
             pltpu.VMEM((rows // 2, kw), f32), pltpu.VMEM((rows // 2, lw), f32), pltpu.VMEM((kw, lw), f32),
-            pltpu.VMEM((2, ny * XC, t, lw), f32),
-            pltpu.VMEM((2, ny, XC, t, lw), f32),
-            pltpu.VMEM((2, nz, XC, t, lw), f32),
+            pltpu.VMEM((2, ny * NEAR, t, lw), f32),
+            pltpu.VMEM((2, ny, NEAR, t, lw), f32),
+            pltpu.VMEM((2, nz, NEAR, t, lw), f32),
             pltpu.VMEM((2 * XC, t, lw), f32),
-            pltpu.VMEM((8, 128), i32), pltpu.VMEM((XC, 8, 128), i32), pltpu.VMEM((nz, 8, 128), i32),
+            pltpu.VMEM((8, 128), i32), pltpu.VMEM((NEAR, 8, 128), i32), pltpu.VMEM((nz, 8, 128), i32),
             pltpu.SMEM((2 * XC,), i32),
             dma((2, CUTS)), dma((2, CUTS)), dma((CUTS,)), dma((CUTS,)), dma, dma, dma, dma,
-            dma((2,)), dma((2, XC)), dma((2,)), dma((2,)), dma, dma,
+            dma((2,)), dma((2, NEAR)), dma((2,)), dma((2,)), dma, dma,
         ],
         name="sketch",
         compiler_params=pltpu.CompilerParams(collective_id=0, has_side_effects=True, vmem_limit_bytes=56 << 20),
     )(slot_image, patch_counts, patches, hidden_grads, proj_in, proj_out)
-    return out.reshape(2 * XC * t, lw)
+    return out.reshape(XC // NEAR, 2 * NEAR * t, lw).sum(0)
 
 
 def solution(mesh):

time: 32.8 us -> 30.3 us (0.924)
  Pallas kernels: 31.3 us -> 29.6 us
  local copies, waits for them, and re-layouts: 1.38 us -> 0 us
  other arithmetic: 0 us -> 0.63 us
    pallas_call x1, Pallas kernels: 31.3 us -> 29.6 us  [body(): pl.pallas_call(functools.partial(kernel, nz, ny), out_shape=pltpu.VMEM((X...]
    unnamed x1 -> x0, local copies, waits for them, and re-layouts: 1.38 us -> none
    reduce_sum x0 -> x1, other arithmetic: none -> 0.63 us  [body(): return out.reshape(XC // NEAR, 2 * NEAR * t, lw).sum(0)]
where the time goes in v3:
time: 30.3 us; the launch traced here: 30.2 us
  Pallas kernels  29.6 us (98%)
  other arithmetic  0.63 us (2%)
    pallas_call x1, Pallas kernels, body(): pl.pallas_call(functools.partial(kernel, nz, ny), out_shape=pltpu.VMEM((X...  29.6 us
    reduce_sum x1, other arithmetic, body(): return out.reshape(XC // NEAR, 2 * NEAR * t, lw).sum(0)  0.63 us

profile of v3, /device:TPU:1, one launch (start us, length us, event | category | flops | bytes accessed | tf_op | source)
XLA Modules:
  0.0 30.2 jit_solution(2210795088119926320)
XLA Ops:
  0.0 29.6 %sketch.1 = f32[4,4,16,128]{3,2,1,0:T(8,128)S(1)} custom-call(s32[2]{0:T(128)} %image_ref.1, s32[2]{0:T(128)} %count_ref.1, bf16[512,6144]{1,0:T(8,128)(2,1)} %x_hbm.1, bf16[512,6144]{1,0:T(8,128)(2,1)} %g_hbm.1, bf16[6144,128]{1,0:T(8,128)(2,1)} %wi_hbm.1, bf16[6144,128]{1,0:T(8,128)(2,1)} %wo_hbm.1), custom_call_target="tpu_custom_call" | custom-call | tf_op jit(solution)/shard_map/sketch/pallas_call | solution.py:295
  29.6 0.6 %reduce_sum.11 = f32[4,16,128]{2,1,0:T(8,128)} reduce(f32[4,4,16,128]{3,2,1,0:T(8,128)S(1)} %sketch.1, f32[]{:T(128)} %constant.0.clone.1), dimensions={0}, to_apply=%region_0.0 | reduce | flops 24576 | bytes 163844 | tf_op jit(solution)/shard_map/reduce_sum | solution.py:316

commit v4 on v3

--- a/solution.py
+++ b/solution.py
@@ -10,7 +10,7 @@
 MESH = pl.DeviceIdType.MESH
 XC = 8
 NEAR = 2
-CUTS = 4
+CUTS = 3
 AHEAD = 3
 
 
@@ -28,9 +28,9 @@
     return hi, lo
 
 
-def kernel(nz, ny, image_ref, count_ref, x_hbm, g_hbm, wi_hbm, wo_hbm, out_ref,
-           xv, gv, wi, wo, red, prj, later, part, gath, ring, pick, idrow, idxc, idz, where_smem,
-           x_sem, g_sem, wi_sem, wo_sem, id_send, id_recv, idz_send, idz_recv,
+def kernel(nz, ny, image_hbm, count_hbm, x_hbm, g_hbm, wi_hbm, wo_hbm, out_ref,
+           xv, gv, wi, wo, red, prj, later, part, gath, ring, pick, idrow, idxc, idz, where_smem, image_ref, count_ref,
+           image_sem, count_sem, x_sem, g_sem, wi_sem, wo_sem, id_send, id_recv, idz_send, idz_recv,
            p1_send, p1_recv, ag_send, ag_recv, p3_send, p3_recv):
     b, y = lax.axis_index("img"), lax.axis_index("hid")
     z, xc = lax.div(b, XC), lax.rem(b, XC)
@@ -82,6 +82,11 @@
         o_in.start()
         g_in.start()
 
+    image_in = pltpu.make_async_copy(image_hbm, image_ref, image_sem)
+    count_in = pltpu.make_async_copy(count_hbm, count_ref, count_sem)
+    image_in.start()
+    count_in.start()
+
     barrier = pltpu.get_barrier_semaphore()
 
     def greet(i, _):
@@ -94,6 +99,10 @@
     for o in range(1, nz):
         pl.semaphore_signal(barrier, inc=1, device_id=at_z(o), device_id_type=MESH)
 
+    later[...] = jnp.zeros_like(later)
+
+    image_in.wait()
+    count_in.wait()
     lane = lax.broadcasted_iota(jnp.int32, (8, 128), 1)
     first, second = image_ref[0], image_ref[1]
     idrow[...] = jnp.where(lane == b, first + 1, jnp.where(lane == slots // 2 + b, second + 1, 0))
@@ -105,13 +114,17 @@
         full = jnp.dot(a, jnp.concatenate([hi, lo], axis=1), preferred_element_type=f32)
         return full[:kw, :lw] + (full[:kw, lw:] + full[kw:, :lw])
 
+    def side_of(yy):
+        return lax.div(yy, 2)
+
+    def quarter(yy):
+        return yy
+
     def send_piece(s, k, yy):
         pltpu.make_async_remote_copy(
-            src_ref=part.at[s, yy * NEAR + k], dst_ref=gath.at[s, y, here],
+            src_ref=part.at[s, quarter(yy) * NEAR + k], dst_ref=gath.at[s, y, here],
             send_sem=p1_send.at[s], recv_sem=p1_recv.at[s, here],
             device_id=(to_near(k), yy), device_id_type=MESH).start()
-
-    later[...] = jnp.zeros_like(later)
 
     def half(h, _):
         def step(q, _):
@@ -157,8 +170,7 @@
         def _():
             pl.semaphore_wait(barrier, ny * XC + nz - 2)
 
-        def to_row(j, _):
-            yy = lax.rem(y + middle_out(j, ny), ny)
+        def to_row(yy, _):
             for o in far_first(NEAR):
                 send_piece(h, near(o), yy)
 
@@ -169,7 +181,7 @@
             return 0
 
         lax.fori_loop(0, ny, to_row, 0)
-        pltpu.make_async_copy(part.at[h, y * NEAR + here], gath.at[h, y, here], p1_recv.at[h, here]).start()
+        pltpu.make_async_copy(part.at[h, quarter(y) * NEAR + here], gath.at[h, y, here], p1_recv.at[h, here]).start()
 
         @pl.when(h == 0)
         def _():
@@ -184,22 +196,25 @@
 
     lax.fori_loop(0, 2, half, 0)
 
+    def others_z(j):
+        return j + jnp.where(j >= z, 1, 0)
+
     def spread(s):
-        def one(j, _):
-            src = near(NEAR - middle_out(NEAR - 1 - j, NEAR))
-            pltpu.make_async_copy(gath.at[s, :, 0], gath.at[s, :, 0], p1_recv.at[s, src]).wait()
-            total = gath[s, 0, src]
-            for i in range(1, ny):
-                total = total + gath[s, i, src]
-            ring[s, z, src] = total
-            for o in far_first(nz):
-                pltpu.make_async_remote_copy(
-                    src_ref=ring.at[s, z, src], dst_ref=ring.at[s, z, src],
-                    send_sem=ag_send.at[s], recv_sem=ag_recv.at[s],
-                    device_id=at_z(o), device_id_type=MESH).start()
+        for k in range(NEAR):
+            pltpu.make_async_copy(gath.at[s, :, 0], gath.at[s, :, 0], p1_recv.at[s, k]).wait()
+        total = gath[s, 0]
+        for i in range(1, ny):
+            total = total + gath[s, i]
+        ring[s, z] = total
+
+        def to_z(j, _):
+            pltpu.make_async_remote_copy(
+                src_ref=ring.at[s, z], dst_ref=ring.at[s, z],
+                send_sem=ag_send.at[s], recv_sem=ag_recv.at[s],
+                device_id=(others_z(j) * XC + xc, y), device_id_type=MESH).start()
             return 0
 
-        lax.fori_loop(0, NEAR, one, 0)
+        lax.fori_loop(0, nz - 1, to_z, 0)
 
     def add_ids(s, _):
         @pl.when(s == 1)
@@ -236,7 +251,7 @@
     for s in range(2):
         pltpu.make_async_copy(ring.at[s, pl.ds(0, nz - 1)], ring.at[s, pl.ds(0, nz - 1)], ag_recv.at[s]).wait()
 
-    side = lax.div(y, 2)
+    side = side_of(y)
     place = lax.rem(y, 2) * NEAR + here
 
     def take(i):
@@ -250,26 +265,22 @@
             src_ref=pick.at[i], dst_ref=out_ref.at[block, place], send_sem=p3_send, recv_sem=p3_recv,
             device_id=(z * XC + cc, yy), device_id_type=MESH).start()
 
-    def to_owner(j, _):
-        cc = at_xc(middle_out(j, XC))
+    def to_owner(cc, _):
         for p in range(2):
-            take(2 * cc + p)
-            deliver(2 * cc + p, cc, 2 * p + side)
+            i, yy = 2 * cc + p, 2 * p + side
+            take(i)
+
+            @pl.when((cc == xc) & (yy == y))
+            def _():
+                pltpu.make_async_copy(pick.at[i], out_ref.at[block, place], p3_recv).start()
+
+            @pl.when((cc != xc) | (yy != y))
+            def _():
+                deliver(i, cc, yy)
+
         return 0
 
-    lax.fori_loop(0, XC - 1, to_owner, 0)
-    for p in range(2):
-        yy = 2 * p + side
-        take(2 * xc + p)
-
-        @pl.when(yy == y)
-        def _():
-            pltpu.make_async_copy(pick.at[2 * xc + p], out_ref.at[block, place], p3_recv).start()
-
-        @pl.when(yy != y)
-        def _():
-            deliver(2 * xc + p, xc, yy)
-
+    lax.fori_loop(0, XC, to_owner, 0)
     for s in range(2):
         sent(ring.at[s, pl.ds(0, nz - 1)], ag_send.at[s])
     own = (y == side) | (y == 2 + side)
@@ -295,7 +306,7 @@
     out = pl.pallas_call(
         functools.partial(kernel, nz, ny),
         out_shape=pltpu.VMEM((XC // NEAR, 2 * NEAR, t, lw), f32),
-        in_specs=[pl.BlockSpec(memory_space=pltpu.SMEM)] * 2 + [pl.BlockSpec(memory_space=pltpu.HBM)] * 4,
+        in_specs=[pl.BlockSpec(memory_space=pltpu.HBM)] * 6,
         out_specs=pl.BlockSpec(memory_space=pltpu.VMEM),
         scratch_shapes=[
             pltpu.VMEM((rows, depth), bf16), pltpu.VMEM((rows, hidden), bf16),
@@ -306,7 +317,7 @@
             pltpu.VMEM((2, nz, NEAR, t, lw), f32),
             pltpu.VMEM((2 * XC, t, lw), f32),
             pltpu.VMEM((8, 128), i32), pltpu.VMEM((NEAR, 8, 128), i32), pltpu.VMEM((nz, 8, 128), i32),
-            pltpu.SMEM((2 * XC,), i32),
+            pltpu.SMEM((2 * XC,), i32), pltpu.SMEM((2,), i32), pltpu.SMEM((2,), i32), dma, dma,
             dma((2, CUTS)), dma((2, CUTS)), dma((CUTS,)), dma((CUTS,)), dma, dma, dma, dma,
             dma((2,)), dma((2, NEAR)), dma((2,)), dma((2,)), dma, dma,
         ],

time: 30.3 us -> 28.8 us (0.950)
  Pallas kernels: 29.6 us -> 28.1 us
    pallas_call x1, Pallas kernels: 29.6 us -> 28.1 us  [body(): pl.pallas_call(functools.partial(kernel, nz, ny), out_shape=pltpu.VMEM((X...]
where the time goes in v4:
time: 28.8 us; the launch traced here: 28.7 us
  Pallas kernels  28.1 us (98%)
  other arithmetic  0.63 us (2%)
    pallas_call x1, Pallas kernels, body(): pl.pallas_call(functools.partial(kernel, nz, ny), out_shape=pltpu.VMEM((X...  28.1 us
    reduce_sum x1, other arithmetic, body(): return out.reshape(XC // NEAR, 2 * NEAR * t, lw).sum(0)  0.63 us

profile of v4, /device:TPU:1, one launch (start us, length us, event | category | flops | bytes accessed | tf_op | source)
XLA Modules:
  0.0 28.7 jit_solution(169105366101841362)
XLA Ops:
  0.0 28.1 %sketch.1 = f32[4,4,16,128]{3,2,1,0:T(8,128)S(1)} custom-call(s32[2]{0:T(128)} %image_hbm.1, s32[2]{0:T(128)} %count_hbm.1, bf16[512,6144]{1,0:T(8,128)(2,1)} %x_hbm.1, bf16[512,6144]{1,0:T(8,128)(2,1)} %g_hbm.1, bf16[6144,128]{1,0:T(8,128)(2,1)} %wi_hbm.1, bf16[6144,128]{1,0:T(8,128)(2,1)} %wo_hbm.1), custom_call_target="tpu_custom_call" | custom-call | tf_op jit(solution)/shard_map/sketch/pallas_call | solution.py:306
  28.1 0.6 %reduce_sum.11 = f32[4,16,128]{2,1,0:T(8,128)} reduce(f32[4,4,16,128]{3,2,1,0:T(8,128)S(1)} %sketch.1, f32[]{:T(128)} %constant.0.clone.1), dimensions={0}, to_apply=%region_0.0 | reduce | flops 24576 | bytes 163844 | tf_op jit(solution)/shard_map/reduce_sum | solution.py:327

commit v5 on v4

--- a/solution.py
+++ b/solution.py
@@ -108,9 +108,9 @@
     idrow[...] = jnp.where(lane == b, first + 1, jnp.where(lane == slots // 2 + b, second + 1, 0))
     c0, c1 = count_ref[0], count_ref[1]
 
-    def sketch(a, h, start, count):
+    def sketch(a, projected, h, start, count):
         pos = lax.broadcasted_iota(jnp.int32, (half_rows, lw), 0) + h * half_rows
-        hi, lo = split(jnp.where((pos >= start) & (pos < start + count), prj[...], 0.0))
+        hi, lo = split(jnp.where((pos >= start) & (pos < start + count), projected, 0.0))
         full = jnp.dot(a, jnp.concatenate([hi, lo], axis=1), preferred_element_type=f32)
         return full[:kw, :lw] + (full[:kw, lw:] + full[kw:, :lw])
 
@@ -127,7 +127,7 @@
             device_id=(to_near(k), yy), device_id_type=MESH).start()
 
     def half(h, _):
-        def step(q, _):
+        def arrive(q):
             for c in rows_in(h, q):
                 c.wait()
 
@@ -150,19 +150,25 @@
                 for c in rows_in(hh, qq):
                     c.start()
 
-            @pl.when(q == 0)
-            def _():
-                red[...] = jnp.zeros_like(red)
-                prj[...] = jnp.zeros_like(prj)
-
+        def products(q):
             r, c = row_part(h), col_part(q)
-            red[...] += jnp.dot(xv[r, c], wi[c, :], preferred_element_type=f32)
-            prj[...] += jnp.dot(gv[r, c], wo[c, :], preferred_element_type=f32)
+            return (
+                red[...] + jnp.dot(xv[r, c], wi[c, :], preferred_element_type=f32),
+                prj[...] + jnp.dot(gv[r, c], wo[c, :], preferred_element_type=f32),
+            )
+
+        def step(q, _):
+            arrive(q)
+            red[...], prj[...] = products(q)
             return 0
 
-        lax.fori_loop(0, CUTS, step, 0)
-        a = jnp.concatenate(split(red[...].T), axis=0)
-        value = later[...] + sketch(a, h, jnp.where(h == 0, 0, c0), jnp.where(h == 0, c0, c1))
+        red[...] = jnp.zeros_like(red)
+        prj[...] = jnp.zeros_like(prj)
+        lax.fori_loop(0, CUTS - 1, step, 0)
+        arrive(CUTS - 1)
+        reduced, projected = products(CUTS - 1)
+        a = jnp.concatenate(split(reduced.T), axis=0)
+        value = later[...] + sketch(a, projected, h, jnp.where(h == 0, 0, c0), jnp.where(h == 0, c0, c1))
         for i in range(npiece):
             part[h, i] = value[i * t : (i + 1) * t]
 
@@ -190,7 +196,7 @@
                     src_ref=idrow, dst_ref=idxc.at[here], send_sem=id_send, recv_sem=id_recv,
                     device_id=(to_near(near(o)), y), device_id_type=MESH).start()
             idxc[here] = idrow[...]
-            later[...] = sketch(a, 0, c0, c1)
+            later[...] = sketch(a, projected, 0, c0, c1)
 
         return 0
 
@@ -265,22 +271,22 @@
             src_ref=pick.at[i], dst_ref=out_ref.at[block, place], send_sem=p3_send, recv_sem=p3_recv,
             device_id=(z * XC + cc, yy), device_id_type=MESH).start()
 
-    def to_owner(cc, _):
-        for p in range(2):
-            i, yy = 2 * cc + p, 2 * p + side
-            take(i)
-
-            @pl.when((cc == xc) & (yy == y))
-            def _():
-                pltpu.make_async_copy(pick.at[i], out_ref.at[block, place], p3_recv).start()
-
-            @pl.when((cc != xc) | (yy != y))
-            def _():
-                deliver(i, cc, yy)
+    def to_owner(n, _):
+        p, cc = lax.div(n, XC), lax.rem(n, XC)
+        i, yy = 2 * cc + p, 2 * p + side
+        take(i)
+
+        @pl.when((cc == xc) & (yy == y))
+        def _():
+            pltpu.make_async_copy(pick.at[i], out_ref.at[block, place], p3_recv).start()
+
+        @pl.when((cc != xc) | (yy != y))
+        def _():
+            deliver(i, cc, yy)
 
         return 0
 
-    lax.fori_loop(0, XC, to_owner, 0)
+    lax.fori_loop(0, 2 * XC, to_owner, 0)
     for s in range(2):
         sent(ring.at[s, pl.ds(0, nz - 1)], ag_send.at[s])
     own = (y == side) | (y == 2 + side)

time: 28.8 us -> 28.8 us (level)
  no operation moved by 1% of the time
where the time goes in v5:
time: 28.8 us; the launch traced here: 28.7 us
  Pallas kernels  28.1 us (98%)
  other arithmetic  0.63 us (2%)
    pallas_call x1, Pallas kernels, body(): pl.pallas_call(functools.partial(kernel, nz, ny), out_shape=pltpu.VMEM((X...  28.1 us
    reduce_sum x1, other arithmetic, body(): return out.reshape(XC // NEAR, 2 * NEAR * t, lw).sum(0)  0.63 us

profile of v5, /device:TPU:1, one launch (start us, length us, event | category | flops | bytes accessed | tf_op | source)
XLA Modules:
  0.0 28.7 jit_solution(9800113702013516727)
XLA Ops:
  0.0 28.1 %sketch.1 = f32[4,4,16,128]{3,2,1,0:T(8,128)S(1)} custom-call(s32[2]{0:T(128)} %image_hbm.1, s32[2]{0:T(128)} %count_hbm.1, bf16[512,6144]{1,0:T(8,128)(2,1)} %x_hbm.1, bf16[512,6144]{1,0:T(8,128)(2,1)} %g_hbm.1, bf16[6144,128]{1,0:T(8,128)(2,1)} %wi_hbm.1, bf16[6144,128]{1,0:T(8,128)(2,1)} %wo_hbm.1), custom_call_target="tpu_custom_call" | custom-call | tf_op jit(solution)/shard_map/sketch/pallas_call | solution.py:312
  28.1 0.6 %reduce_sum.11 = f32[4,16,128]{2,1,0:T(8,128)} reduce(f32[4,4,16,128]{3,2,1,0:T(8,128)S(1)} %sketch.1, f32[]{:T(128)} %constant.0.clone.1), dimensions={0}, to_apply=%region_0.0 | reduce | flops 24576 | bytes 163844 | tf_op jit(solution)/shard_map/reduce_sum | solution.py:333
